TPU v7x, 32 devices: a whole 2x2x4 slice. The times are simulated.
32 devices in a mesh: dp: 8 (over y, x, core), proto: 4 (over z).
Axes of the slice: x: 2, y: 2, z: 4, core: 2. Of those that a mesh axis runs over, the one named last changes fastest.
Arguments:
- features: bfloat16 [4096, 2048], P('dp', 'proto'), may hold values from -8 to 8
- head_weight: bfloat16 [2048, 256], P('proto'), may hold values from -1 to 1
- prototypes: bfloat16 [256, 32768], P(None, 'proto'), may hold values from -1 to 1
Outputs:
- codes: bfloat16 [4096, 32768], P('dp', 'proto')
- proto_grad: float32 [256, 32768], P('dp', 'proto')
- head_grad: float32 [256, 2048], P('dp', 'proto')
All inputs are finite; a program needn't handle non-finite values.
Results may differ from a plain program's by a relative error of at most 0.009.
Values may be sent and summed in bfloat16 or wider, within the bound.
A program may use at most 128 MiB of HBM per device.

v0:
```python
import math

import jax
import jax.numpy as jnp
from jax import lax
from jax.sharding import PartitionSpec as P

PROTOS = 32768
ITERS = 3


sink_eps = 0.05
soft_temp = 0.1


def column_sum(plan):
    return lax.psum(jnp.sum(plan, axis=0), "dp")


def row_sum(plan):
    return lax.psum(jnp.sum(plan, axis=1), "proto")


def on_device(features, head_weight, prototypes):
    partial_proj = jnp.dot(features, head_weight, preferred_element_type=jnp.float32)
    projected = lax.psum(partial_proj, "proto")
    length = jnp.sqrt(jnp.sum(projected * projected, axis=1, keepdims=True) + 1e-06)
    unit = projected / length
    unit_b = unit.astype(jnp.bfloat16)
    proto_f = prototypes.astype(jnp.float32)
    normed = (proto_f / jnp.sqrt(jnp.sum(proto_f * proto_f, axis=0, keepdims=True) + 1e-06)).astype(
        jnp.bfloat16
    )
    scores = jnp.dot(unit_b, normed, preferred_element_type=jnp.float32)
    soft = jnp.exp(scores / soft_temp)
    soft_local = jnp.sum(soft, axis=1)
    plan = jnp.exp(scores / sink_eps)
    for step in range(ITERS):
        plan = plan / column_sum(plan)[None, :]
        plan = plan / row_sum(plan)[:, None]
    soft_total = lax.psum(soft_local, "proto")
    probs = soft / soft_total[:, None]
    codes = (PROTOS * plan).astype(jnp.bfloat16)
    tokens_all = lax.axis_size("dp") * scores.shape[0]
    factor = PROTOS / (soft_temp * math.sqrt(tokens_all))
    dscore = ((probs - plan) * factor).astype(jnp.bfloat16)
    proto_cols = dscore.shape[1]
    dunit_part = lax.dot_general(
        dscore, normed, (((1,), (1,)), ((), ())), preferred_element_type=jnp.float32
    )
    dunit = lax.psum(dunit_part.astype(jnp.bfloat16), "proto").astype(jnp.float32)
    dproj = ((dunit - unit * jnp.sum(unit * dunit, axis=1, keepdims=True)) / length).astype(
        jnp.bfloat16
    )
    head_part = lax.dot_general(
        dproj, features, (((0,), (0,)), ((), ())), preferred_element_type=jnp.float32
    )
    proto_part = lax.dot_general(
        unit_b, dscore, (((0,), (0,)), ((), ())), preferred_element_type=jnp.float32
    )
    summed = lax.psum_scatter(
        jnp.concatenate((proto_part, head_part), axis=1).astype(jnp.bfloat16),
        "dp",
        scatter_dimension=0,
        tiled=True,
    ).astype(jnp.float32)
    proto_grad = summed[:, :proto_cols]
    head_grad = summed[:, proto_cols:]
    return (codes, proto_grad, head_grad)


def solution(mesh):
    in_specs = (P("dp", "proto"), P("proto", None), P(None, "proto"))
    out_specs = (P("dp", "proto"), P("dp", "proto"), P("dp", "proto"))
    return jax.shard_map(
        on_device, mesh=mesh, in_specs=in_specs, out_specs=out_specs, check_vma=False
    )
```

profile of v0, /device:TPU:0, one launch (start us, length us, event | category | flops | bytes accessed | tf_op | source)
XLA Modules:
  0.0 328.3 jit_solution(15468648122413185082)
XLA Ops:
  8.2 2.0 fusion.26
  10.3 3.1 fusion.12
  13.4 38.5 %all-reduce.4.cloned.1.call-done = f32[512,256]{1,0:T(8,128)} async-done(((f32[512,256]{1,0:T(8,128)}), f32[512,256]{1,0:T(8,128)}) %all-reduce.4.cloned.1.call-update) | async-done | bytes 524304 | tf_op jit(solution)/shard_map/psum | solution.py:26
  53.1 11.6 %fusion.14 = (f32[8192]{0:T(1024)S(1)}, f32[512,8192]{1,0:T(8,128)}) fusion(bf16[256,8192]{1,0:T(8,128)(2,1)} %param.5, f32[8192]{0:T(1024)S(1)} %add_sqrt_fusion, f32[512,256]{1,0:T(8,128)} %all-reduce.4.cloned.1.call-done, f32[512]{0:T(512)S(1)} %add_sqrt_fusion.1), kind=kOutput, calls=%fused_computation.24 | convolution fusion | flops 2162417664 | bytes 21563392 | tf_op jit(solution)/shard_map/dot_general | solution.py:34
  64.7 23.3 %psum.64 = f32[8192]{0:T(1024)S(1)} all-reduce(f32[8192]{0:T(1024)S(1)} %get-tuple-element.9), channel_id=1, replica_groups=mesh['dp'=8,'proto'=4] {'dp'}, use_global_device_ids=true, to_apply=%region_4.0 | all-reduce | flops 8192 | bytes 65536 | tf_op jit(solution)/shard_map/psum | solution.py:17
  88.0 8.9 %fusion.11 = (f32[512]{0:T(512)S(1)}, f32[512]{0:T(512)S(1)}) fusion(f32[512,8192]{1,0:T(8,128)} %get-tuple-element.10, f32[8192]{0:T(1024)S(1)} %psum.64), kind=kLoop, calls=%fused_computation.18 | loop fusion | flops 20970496 | bytes 16814080 | tf_op jit(solution)/shard_map/reduce_sum | solution.py:36
  96.9 10.1 %psum.65 = f32[512]{0:T(512)S(1)} all-reduce(f32[512]{0:T(512)S(1)} %get-tuple-element.4), channel_id=1, replica_groups=mesh['dp'=8,'proto'=4] {'proto'}, use_global_device_ids=true, to_apply=%region_6.0 | all-reduce | flops 512 | bytes 4096 | tf_op jit(solution)/shard_map/psum | solution.py:21
  107.1 8.3 %fusion.7 = f32[8192]{0:T(1024)S(1)} fusion(f32[512]{0:T(512)S(1)} %psum.65, f32[8192]{0:T(1024)S(1)} %psum.64, f32[512,8192]{1,0:T(8,128)} %get-tuple-element.10), kind=kLoop, calls=%fused_computation.14 | loop fusion | flops 16769024 | bytes 16844800 | tf_op jit(solution)/shard_map/reduce_sum | solution.py:17
  115.3 22.4 %psum.66 = f32[8192]{0:T(1024)S(1)} all-reduce(f32[8192]{0:T(1024)S(1)} %fusion.7), channel_id=1, replica_groups=mesh['dp'=8,'proto'=4] {'dp'}, use_global_device_ids=true, to_apply=%region_8.0 | all-reduce | flops 8192 | bytes 65536 | tf_op jit(solution)/shard_map/psum | solution.py:17
  137.7 8.3 %fusion.8 = f32[512]{0:T(512)S(1)} fusion(f32[8192]{0:T(1024)S(1)} %psum.66, f32[512]{0:T(512)S(1)} %psum.65, f32[8192]{0:T(1024)S(1)} %psum.64, f32[512,8192]{1,0:T(8,128)} %get-tuple-element.10), kind=kLoop, calls=%fused_computation.15 | loop fusion | flops 20971008 | bytes 16846848 | tf_op jit(solution)/shard_map/reduce_sum | solution.py:21
  146.0 8.6 %psum.67 = f32[512]{0:T(512)S(1)} all-reduce(f32[512]{0:T(512)S(1)} %fusion.8), channel_id=1, replica_groups=mesh['dp'=8,'proto'=4] {'proto'}, use_global_device_ids=true, to_apply=%region_10.0 | all-reduce | flops 512 | bytes 4096 | tf_op jit(solution)/shard_map/psum | solution.py:21
  154.6 8.6 %fusion.9 = f32[8192]{0:T(1024)S(1)} fusion(f32[512]{0:T(512)S(1)} %psum.67, f32[8192]{0:T(1024)S(1)} %psum.66, f32[512]{0:T(512)S(1)} %psum.65, f32[8192]{0:T(1024)S(1)} %psum.64, f32[512,8192]{1,0:T(8,128)} %get-tuple-element.10), kind=kLoop, calls=%fused_computation.16 | loop fusion | flops 25157632 | bytes 16879616 | tf_op jit(solution)/shard_map/reduce_sum | solution.py:17
  163.2 22.5 %psum.68 = f32[8192]{0:T(1024)S(1)} all-reduce(f32[8192]{0:T(1024)S(1)} %fusion.9), channel_id=1, replica_groups=mesh['dp'=8,'proto'=4] {'dp'}, use_global_device_ids=true, to_apply=%region_12.0 | all-reduce | flops 8192 | bytes 65536 | tf_op jit(solution)/shard_map/psum | solution.py:17
  185.7 9.0 %fusion.10 = f32[512]{0:T(512)S(1)} fusion(f32[8192]{0:T(1024)S(1)} %psum.68, f32[512]{0:T(512)S(1)} %psum.67, f32[8192]{0:T(1024)S(1)} %psum.66, f32[512]{0:T(512)S(1)} %psum.65, f32[8192]{0:T(1024)S(1)} %psum.64, f32[512,8192]{1,0:T(8,128)} %get-tuple-element.10), kind=kLoop, calls=%fused_computation.17 | loop fusion | flops 29359616 | bytes 16881664 | tf_op jit(solution)/shard_map/reduce_sum | solution.py:21
  194.7 10.1 %all-reduce = (f32[512]{0:T(512)S(1)}, f32[512]{0:T(512)S(1)}) all-reduce(f32[512]{0:T(512)S(1)} %fusion.10, f32[512]{0:T(512)S(1)} %get-tuple-element.3), channel_id=1, replica_groups=mesh['dp'=8,'proto'=4] {'proto'}, use_global_device_ids=true, to_apply=%region_14.0 | all-reduce | flops 1024 | bytes 8192 | tf_op jit(solution)/shard_map/psum | solution.py:21
  204.9 14.9 %multiply_convert_fusion = (bf16[512,8192]{1,0:T(8,128)(2,1)S(1)}, bf16[512,8192]{1,0:T(8,128)(2,1)}) fusion(f32[512,8192]{1,0:T(8,128)} %get-tuple-element.10, f32[512]{0:T(512)S(1)} %get-tuple-element.6, f32[512]{0:T(512)S(1)} %get-tuple-element.5, f32[8192]{0:T(1024)S(1)} %psum.68, f32[512]{0:T(512)S(1)} %psum.67, f32[8192]{0:T(1024)S(1)} %psum.66, ...), kind=kLoop, calls=%fused_computation.9 | loop fusion | flops 58720256 | bytes 33660928 | tf_op jit(solution)/shard_map/convert_element_type | solution.py:46
  219.8 3.2 copy-done.1
  223.0 3.1 convolution_convert_fusion.2
  226.2 7.9 %convolution_convert_fusion = bf16[256,8192]{1,0:T(8,128)(2,1)} fusion(bf16[512,8192]{1,0:T(8,128)(2,1)} %copy-done.1, f32[512,256]{1,0:T(8,128)S(1)} %copy-done.2, f32[512]{0:T(512)S(1)} %add_sqrt_fusion.1), kind=kOutput, calls=%fused_computation.21 | convolution fusion | flops 2149842944 | bytes 13109248 | tf_op jit(solution)/shard_map/dot_general | solution.py:58
  234.0 24.4 %all-reduce.6.cloned.1.call-done = bf16[512,256]{1,0:T(8,128)(2,1)} async-done(((bf16[512,256]{1,0:T(8,128)(2,1)}), bf16[512,256]{1,0:T(8,128)(2,1)}) %all-reduce.6.cloned.1.call-update) | async-done | bytes 262160 | tf_op jit(solution)/shard_map/psum | solution.py:51
  259.7 1.5 convolution_convert_fusion.1
  261.2 4.5 %pad_maximum_fusion = bf16[256,8704]{1,0:T(8,128)(2,1)} fusion(bf16[256,512]{1,0:T(8,128)(2,1)S(1)} %convolution_convert_fusion.1, bf16[256,8192]{1,0:T(8,128)(2,1)} %convolution_convert_fusion), kind=kLoop, calls=%fused_computation.25 | loop fusion | flops 8912896 | bytes 8912896 | tf_op jit(solution)/shard_map/concatenate | solution.py:62
  265.7 52.6 %reduce-scatter.2.cloned.1.call-done = bf16[32,8704]{1,0:T(8,128)(2,1)} async-done(((bf16[256,8704]{1,0:T(8,128)(2,1)}), bf16[32,8704]{1,0:T(8,128)(2,1)}) %reduce-scatter.2.cloned.1.call-update) | async-done | bytes 557072 | tf_op jit(solution)/shard_map/reduce_scatter | solution.py:61
  319.7 2.1 slice.8
  (18 shorter events, 5.0 us)
Async XLA Ops:
  7.2 1.0 copy-start
  7.2 44.8 %all-reduce.4.cloned.1.call-start = ((), (), s32[]{:S(2)}) async-start(), calls=%async_computation.1 | async-start | bytes 1048576 | tf_op jit(solution)/shard_map/psum | solution.py:26
  10.3 248.2 %all-reduce.6.cloned.1.call-start = ((), (), s32[]{:S(2)}) async-start(), calls=%async_computation.2 | async-start | bytes 524288 | tf_op jit(solution)/shard_map/psum | solution.py:51
  204.9 18.1 %copy-start.3 = (bf16[256,8192]{1,0:T(8,128)(2,1)S(1)}, bf16[256,8192]{1,0:T(8,128)(2,1)}, u32[]{:S(2)}) copy-start(bf16[256,8192]{1,0:T(8,128)(2,1)} %param.5) | copy-start | bytes 12582916
  219.8 3.2 copy-start.1
  223.0 3.2 copy-start.2
  226.1 92.2 %reduce-scatter.2.cloned.1.call-start = ((), (), s32[]{:S(2)}) async-start(), calls=%async_computation.3 | async-start | bytes 5013504 | tf_op jit(solution)/shard_map/reduce_scatter | solution.py:61
Sparse Core Ops, SparseCore 0:
  10.9 40.9 all-reduce.3
  226.2 32.2 all-reduce.5
  265.9 52.4 reduce-scatter.1
where the time goes:
time: 329 us; the launch traced here: 328 us
  waiting for transfers between devices  116 us (35%)
  blocking collectives  97.1 us (30%)
  other arithmetic  68 us (21%)
  matrix products  26.1 us (8%)
  between operations  13.8 us (4%)
  local copies, waits for them, and re-layouts  7.69 us (2%)
    psum x3, blocking collectives, column_sum(): return lax.psum(jnp.sum(plan, axis=0), 'dp')  68.2 us
    reduce_scatter x1, waiting for transfers between devices, on_device(): lax.psum_scatter(jnp.concatenate((proto_part, head_part), axis=1).astype(...  52.6 us
    psum x1, waiting for transfers between devices, on_device(): projected = lax.psum(partial_proj, 'proto')  38.5 us
    psum x3, blocking collectives, row_sum(): return lax.psum(jnp.sum(plan, axis=1), 'proto')  28.9 us
    psum x1, waiting for transfers between devices, on_device(): lax.psum(dunit_part.astype(jnp.bfloat16), 'proto').astype(jnp.float32)  24.4 us
    reduce_sum x2, other arithmetic, row_sum(): return lax.psum(jnp.sum(plan, axis=1), 'proto')  17.3 us
    reduce_sum x2, other arithmetic, column_sum(): return lax.psum(jnp.sum(plan, axis=0), 'dp')  16.8 us
    convert_element_type x1, other arithmetic, on_device(): dscore = ((probs - plan) * factor).astype(jnp.bfloat16)  14.9 us
  transfers between devices with their start and end apart: 3, of which 3 were waited for; matrix products, arithmetic and copies ran while one was open for 3% of the time, Pallas kernels for 0%

commit v1 on v0

v1 whole, which is shorter than its diff:
```python
import functools
import math

import jax
import jax.numpy as jnp
from jax import lax
from jax.experimental import pallas as pl
from jax.experimental.pallas import tpu as pltpu
from jax.sharding import PartitionSpec as P

PROTOS = 32768
ITERS = 3
SOFT_TEMP = 0.1
CHUNKS = 4
F32 = jnp.float32
BF16 = jnp.bfloat16


def kernel(D, Z, f_ref, w_ref, p_ref, codes_ref, pg_ref, hg_ref,
           nb, S, cs, c8, racc, rcol, tcol, psend, precv, ub, ubt, unit_s, len_s,
           colsend, colrecv, rsend, rrecv, cst, dbuf, dacc, dusend, durecv, dpall,
           gsend, garecv, gbrecv,
           psem_s, psem_r, usem_s, usem_r, csem_s, csem_r, rsem_s, rsem_r,
           dsem_s, dsem_r, hsem_s, hsem_r, asem_s, asem_r, bsem_s, bsem_r, osem):
    T, FI = f_ref.shape
    EMB, N = p_ref.shape
    R = T // Z
    H = D // 2
    ROWS = EMB // D
    CW = N // CHUNKS
    md = lax.axis_index("dp")
    mz = lax.axis_index("proto")
    mc = lax.rem(md, 2)
    chip = md // 2
    pc = 1 - mc

    def zpeer(k):
        return lax.rem(mz + k, Z)

    def dpeer(k):
        return lax.rem(md + k, D)

    def remote(src, dst, s, r, **dev):
        return pltpu.make_async_remote_copy(
            src_ref=src, dst_ref=dst, send_sem=s, recv_sem=r,
            device_id=dev, device_id_type=pl.DeviceIdType.MESH)

    barrier = pltpu.get_barrier_semaphore()
    for k in range(1, D):
        pl.semaphore_signal(barrier, inc=1, device_id={"dp": dpeer(k)},
                            device_id_type=pl.DeviceIdType.MESH)
    for k in range(1, Z):
        pl.semaphore_signal(barrier, inc=1, device_id={"proto": zpeer(k)},
                            device_id_type=pl.DeviceIdType.MESH)

    for b in range(Z):
        psend[b] = jnp.dot(f_ref[b * R:(b + 1) * R, :], w_ref[...],
                           preferred_element_type=F32).astype(BF16)
    pl.semaphore_wait(barrier, D + Z - 2)

    sends = []
    pcs = []
    for k in range(1, Z):
        cp = remote(psend.at[zpeer(k)], precv.at[k - 1], psem_s.at[k - 1], psem_r.at[k - 1],
                    proto=zpeer(k))
        cp.start()
        pcs.append(cp)
    sends += pcs

    NB = 256

    @pl.loop(0, N // NB)
    def _(j):
        cols = pl.ds(pl.multiple_of(j * NB, NB), NB)
        sq = jnp.zeros((8, NB), F32)
        for g in range(EMB // 32):
            x = p_ref[g * 32:(g + 1) * 32, cols].astype(F32)
            x = x * x
            sq = sq + ((x[0:8] + x[8:16]) + (x[16:24] + x[24:32]))
        inv = 1.0 / jnp.sqrt(jnp.sum(sq, axis=0, keepdims=True) + 1e-06)
        for g in range(EMB // 32):
            x = p_ref[g * 32:(g + 1) * 32, cols].astype(F32)
            nb[g * 32:(g + 1) * 32, cols] = (x * inv).astype(BF16)
        cs[:, cols] = jnp.zeros((8, NB), F32)

    myrows = pl.ds(pl.multiple_of(mz * R, R), R)
    proj = jnp.dot(f_ref[myrows, :], w_ref[...], preferred_element_type=F32)
    for cp in pcs:
        cp.wait_recv()
    for k in range(1, Z):
        proj = proj + precv[k - 1].astype(F32)
    length = jnp.sqrt(jnp.sum(proj * proj, axis=1, keepdims=True) + 1e-06)
    unit = proj / length
    unit_s[...] = unit
    len_s[...] = jnp.broadcast_to(length, (R, 128))
    ub[myrows, :] = unit.astype(BF16)
    ucs = []
    for k in range(1, Z):
        cp = remote(ub.at[myrows, :], ub.at[myrows, :], usem_s.at[k - 1], usem_r.at[k - 1],
                    proto=zpeer(k))
        cp.start()
        ucs.append(cp)
    sends += ucs

    SB = 512

    def score_rows(z):
        rows = pl.ds(pl.multiple_of(z * R, R), R)
        u = ub[rows, :]

        def body(j, acc):
            cols = pl.ds(pl.multiple_of(j * SB, SB), SB)
            s = jnp.dot(u, nb[:, cols], preferred_element_type=F32)
            e = jnp.exp(s * (1.0 / SOFT_TEMP))
            S[rows, cols] = e
            e2 = e * e
            cs[:, cols] += jnp.sum(e2.reshape(R // 8, 8, SB), axis=0)
            for i in range(SB // 128):
                acc = acc + e[:, i * 128:(i + 1) * 128]
            return acc

        racc[rows, :] = lax.fori_loop(0, N // SB, body, jnp.zeros((R, 128), F32))

    for k in range(Z):
        if k:
            ucs[k - 1].wait_recv()
        score_rows(lax.rem(mz + Z - k, Z))

    def start_rows(it):
        v = jnp.sum(jnp.transpose(racc[...]), axis=0, keepdims=True)
        rsend[it] = v
        out = []
        for k in range(1, Z):
            cp = remote(rsend.at[it], rrecv.at[it, k - 1], rsem_s.at[it, k - 1],
                        rsem_r.at[it, k - 1], proto=zpeer(k))
            cp.start()
            out.append(cp)
        return out

    def end_rows(it, cps):
        for cp in cps:
            cp.wait_recv()
        v = rsend[it]
        for k in range(1, Z):
            v = v + rrecv[it, k - 1]
        return 1.0 / v

    def to_col(v):
        return jnp.transpose(jnp.broadcast_to(v, (128, T)))

    def start_cols(it):
        colsend[it] = jnp.sum(cs[...], axis=0, keepdims=True)
        out = []
        for k in range(1, D):
            cp = remote(colsend.at[it], colrecv.at[it, k - 1], csem_s.at[it, k - 1],
                        csem_r.at[it, k - 1], dp=dpeer(k))
            cp.start()
            out.append(cp)
        return out

    def end_cols(it, cps):
        for cp in cps:
            cp.wait_recv()
        v = colsend[it]
        for k in range(1, D):
            v = v + colrecv[it, k - 1]
        c8[...] = jnp.broadcast_to(1.0 / v, (8, N))

    def row_pass():
        G = 64

        @pl.loop(0, T // G)
        def _(g):
            rows = pl.ds(pl.multiple_of(g * G, G), G)

            def body(j, acc):
                for i in range(8):
                    cols = pl.ds(pl.multiple_of(j * 1024 + i * 128, 128), 128)
                    c = c8[:, cols]
                    new = []
                    for q in range(G // 8):
                        x = S[pl.ds(pl.multiple_of(g * G + q * 8, 8), 8), cols]
                        new.append(acc[q] + x * x * c)
                    acc = tuple(new)
                return acc

            acc = lax.fori_loop(0, N // 1024, body,
                                tuple(jnp.zeros((8, 128), F32) for _ in range(G // 8)))
            racc[rows, :] = jnp.concatenate(acc, axis=0)

    def col_pass():
        W = 1024

        @pl.loop(0, N // W)
        def _(j):
            def body(g, acc):
                for q in range(8):
                    rows = pl.ds(pl.multiple_of(g * 64 + q * 8, 8), 8)
                    r = rcol[rows, :]
                    new = []
                    for i in range(W // 128):
                        x = S[rows, pl.ds(pl.multiple_of(j * W + i * 128, 128), 128)]
                        new.append(acc[i] + x * x * r)
                    acc = tuple(new)
                return acc

            acc = lax.fori_loop(0, T // 64, body,
                                tuple(jnp.zeros((8, 128), F32) for _ in range(W // 128)))
            cs[:, pl.ds(pl.multiple_of(j * W, W), W)] = jnp.concatenate(acc, axis=1)

    soft_cps = None
    kf = 1.0 / (SOFT_TEMP * math.sqrt(D * T))
    for it in range(ITERS):
        cps = start_cols(it)
        sends += cps
        if it == 0:
            soft_cps = start_rows(ITERS)
            sends += soft_cps
            ubt[...] = jnp.transpose(ub[...].astype(F32)).astype(BF16)
        end_cols(it, cps)
        row_pass()
        cps = start_rows(it)
        sends += cps
        if it == 0:
            tcol[...] = to_col(end_rows(ITERS, soft_cps) * (PROTOS * kf))
        inv = end_rows(it, cps)
        if it < ITERS - 1:
            rcol[...] = to_col(inv)
            col_pass()
        else:
            rcol[...] = to_col(inv * PROTOS)

    FB = 256
    dacc[...] = jnp.zeros_like(dacc)

    def chunk_cols(q):
        return (pl.ds(q * CW, CW) if q < CHUNKS else pl.ds(N, FI))

    def start_a(q):
        cols = chunk_cols(q)
        cp = remote(gsend.at[pl.ds(pc * H, H), :, cols], garecv.at[:, :, cols],
                    asem_s.at[q], asem_r.at[q], dp=md + 1 - 2 * mc)
        cp.start()
        sends.append(cp)
        return cp

    def start_b(q, cpa):
        cpa.wait_recv()
        cols = chunk_cols(q)

        @pl.loop(0, H)
        def _(k):
            gsend[mc * H + k, :, cols] = (gsend[mc * H + k, :, cols].astype(F32)
                                          + garecv[k, :, cols].astype(F32)).astype(BF16)

        out = []
        for k in range(1, H):
            dst = lax.rem(chip + k, H)
            cp = remote(gsend.at[mc * H + dst, :, cols], gbrecv.at[k - 1, :, cols],
                        bsem_s.at[q, k - 1], bsem_r.at[q, k - 1], dp=dst * 2 + mc)
            cp.start()
            out.append(cp)
        sends.extend(out)
        return out

    def finish(q, cps):
        for cp in cps:
            cp.wait_recv()
        cols = chunk_cols(q)
        v = gsend[mc * H + chip, :, cols].astype(F32)
        for k in range(1, H):
            v = v + gbrecv[k - 1, :, cols].astype(F32)
        if q < CHUNKS:
            pg_ref[:, cols] = v
        else:
            hg_ref[...] = v

    outs = []
    acp = []
    bcp = []
    for q in range(CHUNKS):
        slot = q % 2
        if q >= 2:
            outs[q - 2].wait()

        @pl.loop(0, CW // FB)
        def _(j, q=q, slot=slot):
            lcols = pl.ds(pl.multiple_of(j * FB, FB), FB)
            cols = pl.ds(pl.multiple_of(q * CW + j * FB, FB), FB)
            c = c8[:, cols][0:1, :]

            @pl.loop(0, T // 32)
            def _(g):
                rows = pl.ds(pl.multiple_of(g * 32, 32), 32)
                x = S[rows, cols]
                r = rcol[rows, :]
                t = tcol[rows, :]
                r = jnp.concatenate([r] * (FB // 128), axis=1)
                t = jnp.concatenate([t] * (FB // 128), axis=1)
                plan = x * x * c * r
                cst[slot, rows, lcols] = plan.astype(BF16)
                dbuf[rows, :] = (x * t - plan * kf).astype(BF16)

            d = dbuf[...]
            dacc[...] += lax.dot_general(d, nb[:, cols], (((1,), (1,)), ((), ())),
                                         preferred_element_type=F32)
            res = jnp.dot(ubt[...], d, preferred_element_type=F32).astype(BF16)
            for e in range(D):
                gsend[(e % 2) * H + e // 2, :, cols] = res[e * ROWS:(e + 1) * ROWS, :]

        cp = pltpu.make_async_copy(cst.at[slot], codes_ref.at[:, pl.ds(q * CW, CW)], osem.at[q])
        cp.start()
        outs.append(cp)
        acp.append(start_a(q))
        if q == CHUNKS - 1:
            for b in range(Z):
                dusend[b] = dacc[b * R:(b + 1) * R, :].astype(BF16)
            dcs = []
            for k in range(1, Z):
                cp = remote(dusend.at[zpeer(k)], durecv.at[k - 1], dsem_s.at[k - 1],
                            dsem_r.at[k - 1], proto=zpeer(k))
                cp.start()
                dcs.append(cp)
            sends += dcs
        if q >= 1:
            bcp.append(start_b(q - 1, acp[q - 1]))

    du = dacc[myrows, :]
    for cp in dcs:
        cp.wait_recv()
    for k in range(1, Z):
        du = du + durecv[k - 1].astype(F32)
    unit = unit_s[...]
    dp = (du - unit * jnp.sum(unit * du, axis=1, keepdims=True)) / len_s[:, 0:1]
    dpall[myrows, :] = dp.astype(BF16)
    hcs = []
    for k in range(1, Z):
        cp = remote(dpall.at[myrows, :], dpall.at[myrows, :], hsem_s.at[k - 1], hsem_r.at[k - 1],
                    proto=zpeer(k))
        cp.start()
        hcs.append(cp)
    sends += hcs
    bcp.append(start_b(CHUNKS - 1, acp[CHUNKS - 1]))
    for cp in hcs:
        cp.wait_recv()
    dpt = jnp.transpose(dpall[...].astype(F32)).astype(BF16)
    res = jnp.dot(dpt, f_ref[...], preferred_element_type=F32).astype(BF16)
    for e in range(D):
        gsend[(e % 2) * H + e // 2, :, N:N + FI] = res[e * ROWS:(e + 1) * ROWS, :]
    acp.append(start_a(CHUNKS))
    bcp.append(start_b(CHUNKS, acp[CHUNKS]))
    for q in range(CHUNKS + 1):
        finish(q, bcp[q])
    for cp in outs[-2:]:
        cp.wait()
    for cp in sends:
        cp.wait_send()


def solution(mesh):
    D, Z = mesh.shape["dp"], mesh.shape["proto"]

    def on_device(features, head_weight, prototypes):
        T, FI = features.shape
        EMB, N = prototypes.shape
        R, H, ROWS, C = T // Z, D // 2, EMB // D, N + FI
        V = pltpu.VMEM
        dma = pltpu.SemaphoreType.DMA
        vspec = pl.BlockSpec(memory_space=pltpu.VMEM)
        return pl.pallas_call(
            functools.partial(kernel, D, Z),
            out_shape=(
                jax.ShapeDtypeStruct((T, N), BF16),
                jax.ShapeDtypeStruct((ROWS, N), F32),
                jax.ShapeDtypeStruct((ROWS, FI), F32),
            ),
            in_specs=[vspec] * 3,
            out_specs=(pl.BlockSpec(memory_space=pl.ANY), vspec, vspec),
            scratch_shapes=[
                V((EMB, N), BF16), V((T, N), F32), V((8, N), F32), V((8, N), F32),
                V((T, 128), F32), V((T, 128), F32), V((T, 128), F32),
                V((Z, R, EMB), BF16), V((Z - 1, R, EMB), BF16),
                V((T, EMB), BF16), V((EMB, T), BF16), V((R, EMB), F32), V((R, 128), F32),
                V((ITERS, 1, N), F32), V((ITERS, D - 1, 1, N), F32),
                V((ITERS + 1, 1, T), F32), V((ITERS + 1, Z - 1, 1, T), F32),
                V((2, T, N // CHUNKS), BF16), V((T, 256), BF16), V((T, EMB), F32),
                V((Z, R, EMB), BF16), V((Z - 1, R, EMB), BF16), V((T, EMB), BF16),
                V((D, ROWS, C), BF16), V((H, ROWS, C), BF16), V((H - 1, ROWS, C), BF16),
                dma((Z - 1,)), dma((Z - 1,)), dma((Z - 1,)), dma((Z - 1,)),
                dma((ITERS, D - 1)), dma((ITERS, D - 1)),
                dma((ITERS + 1, Z - 1)), dma((ITERS + 1, Z - 1)),
                dma((Z - 1,)), dma((Z - 1,)), dma((Z - 1,)), dma((Z - 1,)),
                dma((CHUNKS + 1,)), dma((CHUNKS + 1,)),
                dma((CHUNKS + 1, H - 1)), dma((CHUNKS + 1, H - 1)),
                dma((CHUNKS,)),
            ],
            compiler_params=pltpu.CompilerParams(
                collective_id=0, has_side_effects=True, vmem_limit_bytes=60 * 1024 * 1024),
            cost_estimate=pl.CostEstimate(
                flops=6 * T * N * EMB, bytes_accessed=16 * 1024 * 1024,
                transcendentals=T * N),
        )(features, head_weight, prototypes)

    return jax.shard_map(
        on_device, mesh=mesh,
        in_specs=(P("dp", "proto"), P("proto", None), P(None, "proto")),
        out_specs=(P("dp", "proto"), P("dp", "proto"), P("dp", "proto")),
        check_vma=False)
```

time: 329 us -> 130 us (0.40)
  Pallas kernels: 0 us -> 119 us
  waiting for transfers between devices: 116 us -> 0 us
  blocking collectives: 97.1 us -> 0 us
  other arithmetic: 68 us -> 0 us
  matrix products: 26.1 us -> 0 us
  between operations: 13.8 us -> 0.66 us
    pallas_call x0 -> x1, Pallas kernels: none -> 119 us  [on_device(): pl.pallas_call(functools.partial(kernel, D, Z), out_shape=(jax.ShapeDtype...]
    psum x6 -> x0, blocking collectives: 97.1 us -> none  [the longest x3 68.2 us: column_sum(): return lax.psum(jnp.sum(plan, axis=0), 'dp')]
    psum x2 -> x0, waiting for transfers between devices: 63 us -> none  [the longest x1 38.5 us: on_device(): projected = lax.psum(partial_proj, 'proto')]
    reduce_scatter x1 -> x0, waiting for transfers between devices: 52.6 us -> none  [on_device(): lax.psum_scatter(jnp.concatenate((proto_part, head_part), axis=1).astype(...]
    reduce_sum x8 -> x0, other arithmetic: 48.5 us -> none  [the longest x2 17.3 us: row_sum(): return lax.psum(jnp.sum(plan, axis=1), 'proto')]
    dot_general x5 -> x0, matrix products: 26.1 us -> none  [the longest x1 11.6 us: on_device(): scores = jnp.dot(unit_b, normed, preferred_element_type=jnp.float32)]
    convert_element_type x1 -> x0, other arithmetic: 14.9 us -> none  [on_device(): dscore = ((probs - plan) * factor).astype(jnp.bfloat16)]
    unnamed x8 -> x7, local copies, waits for them, and re-layouts: 4.22 us -> 9.47 us
  transfers between devices with their start and end apart: 3 -> 0, of which waited for: 3 -> 0; matrix products, arithmetic and copies ran while one was open for 3% -> 0% of each run, Pallas kernels for 0% -> 0%
where the time goes in v1:
time: 130 us
  Pallas kernels  119 us (92%)
  local copies, waits for them, and re-layouts  9.47 us (7%)
    pallas_call x1, Pallas kernels, on_device(): pl.pallas_call(functools.partial(kernel, D, Z), out_shape=(jax.ShapeDtype...  119 us
    unnamed x7, local copies, waits for them, and re-layouts  9.47 us

profile of v1, /device:TPU:0, one launch (start us, length us, event | category | flops | bytes accessed | tf_op | source)
XLA Modules:
  0.0 129.6 jit_solution(16868078317568727560)
XLA Ops:
  0.6 119.5 %shard_map.58 = (bf16[512,8192]{1,0:T(8,128)(2,1)}, f32[32,8192]{1,0:T(8,128)}, f32[32,512]{1,0:T(8,128)}) custom-call(bf16[512,512]{1,0:T(8,128)(2,1)} %f_ref.1, bf16[512,256]{1,0:T(8,128)(2,1)} %w_ref.1, bf16[256,8192]{1,0:T(8,128)(2,1)} %p_ref.1), custom_call_target="tpu_custom_call" | custom-call | flops 6442450944 | bytes 16777216 | tf_op jit(solution)/shard_map/pallas_call | solution.py:370
  120.1 0.0 copy-start
  120.1 0.0 copy-start.1
  120.2 7.9 %copy.9 = bf16[512,8192]{1,0:T(8,128)(2,1)} copy(bf16[512,8192]{1,0:T(8,128)(2,1)} %get-tuple-element.6) | data formatting | bytes 16777216
  128.0 0.0 copy-done
  128.0 1.0 copy.10
  129.0 0.0 copy-done.1
  129.0 0.6 copy.11
Async XLA Ops:
  120.1 7.9 %copy-start = (f32[32,8192]{1,0:T(8,128)S(1)}, f32[32,8192]{1,0:T(8,128)}, u32[]{:S(2)}) copy-start(f32[32,8192]{1,0:T(8,128)} %get-tuple-element.7) | copy-start | bytes 3145732
  120.1 8.8 %copy-start.1 = (f32[32,512]{1,0:T(8,128)S(1)}, f32[32,512]{1,0:T(8,128)}, u32[]{:S(2)}) copy-start(f32[32,512]{1,0:T(8,128)} %get-tuple-element.8) | copy-start | bytes 196612
